TPU v7x, 256 devices: a whole 4x4x8 slice. The times are simulated.
256 devices in a mesh: fsdp: 64 (over y, z_lo, x, core), ctx: 4 (over z_hi).
Axes of the slice: x: 4, y: 4, z: 8 (z_hi: 4, z_lo: 2; z = z_hi * 2 + z_lo), core: 2. Of those that a mesh axis runs over, the one named last changes fastest.
Arguments:
- q_feat: bfloat16 [64, 512, 4096], P('fsdp', 'ctx'), may hold values from -6 to 6
- k_feat: bfloat16 [64, 512, 4096], P('fsdp', 'ctx'), may hold values from -6 to 6
- v_feat: bfloat16 [64, 512, 4096], P('fsdp', 'ctx'), may hold values from -6 to 6
- residue: float32 [4096, 16], P('ctx'), may hold values from -0.125 to 0.125
- rate: float32 [4096, 16], P('ctx'), may hold values from 0.00048828125 to 0.04
- w_out: bfloat16 [4096, 4096], P('fsdp', 'ctx'), may hold values from -0.09375 to 0.09375
- cotangent: bfloat16 [64, 512, 4096], P('fsdp', 'ctx')
Outputs:
- grad_q: bfloat16 [64, 512, 4096], P('fsdp', 'ctx')
- grad_k: bfloat16 [64, 512, 4096], P('fsdp', 'ctx')
- grad_v: bfloat16 [64, 512, 4096], P('fsdp', 'ctx')
- grad_weight: float32 [4096, 4096], P('fsdp', 'ctx')
- grad_residue: float32 [4096, 16], P('ctx')
- grad_rate: float32 [4096, 16], P('ctx')
All inputs are finite; a program needn't handle non-finite values.
Results may differ from a plain program's by a relative error of at most 0.008.
Values may be sent and summed in bfloat16 or wider, within the bound.
A program may use at most 128 MiB of HBM per device.

v0:
```python
import jax
import jax.numpy as jnp
from jax import lax
from jax.sharding import PartitionSpec as P


def dft_tables(length):
    indices = jnp.arange(length, dtype=jnp.int32)
    product_mod = indices[:, None] * indices[None, :] % (2 * length)
    angles = jnp.pi * product_mod.astype(jnp.float32) / length
    cosine = jnp.cos(angles).astype(jnp.bfloat16)
    sine_table = jnp.sin(angles).astype(jnp.bfloat16)
    parity = jnp.where(indices % 2 == 0, 1.0, -1.0).astype(jnp.float32)
    return (cosine, sine_table, parity)


def filter_spectrum(residue, rate, length):
    indices = jnp.arange(length + 1, dtype=jnp.int32)
    angle_step = jnp.pi * indices.astype(jnp.float32) / length
    parity = jnp.where(indices % 2 == 0, 1.0, -1.0).astype(jnp.float32)[:, None, None]
    retained = jnp.exp(-rate)[None]
    margin = -jnp.expm1(-rate)[None]
    ending = jnp.exp(-rate * length)[None]
    half_sin = jnp.sin(0.5 * angle_step)[:, None, None]
    across = margin + 2.0 * retained * half_sin * half_sin
    upward = retained * jnp.sin(angle_step)[:, None, None]
    weights = residue[None] * (1.0 - ending * parity) / (across * across + upward * upward)
    real_part = jnp.sum(weights * across, axis=2)
    imag_part = -jnp.sum(weights * upward, axis=2)
    return (real_part[:length], imag_part[:length], real_part[length])


def to_spectrum(cosine, sine_table, parity, signal):
    row_count = signal.shape[0]
    stacked = jnp.concatenate([cosine, sine_table], axis=0)
    product = jnp.dot(stacked, signal, preferred_element_type=jnp.float32)
    nyquist = jnp.dot(
        parity.astype(jnp.bfloat16)[None, :], signal, preferred_element_type=jnp.float32
    )[0]
    return (product[:row_count], -product[row_count:], nyquist)


def from_spectrum(cosine, sine_table, parity, real_part, imag_part, nyquist):
    row_count = real_part.shape[0]
    doubling = jnp.where(jnp.arange(row_count) == 0, 1.0, 2.0).astype(jnp.float32)[:, None]
    packed = jnp.concatenate([real_part * doubling, -(imag_part * doubling)], axis=0).astype(
        jnp.bfloat16
    )
    wide_table = jnp.concatenate([cosine, sine_table], axis=1)
    summed = jnp.dot(wide_table, packed, preferred_element_type=jnp.float32)
    return (summed + parity[:, None] * nyquist[None, :]) / (2.0 * row_count)


def shards(q_feat, k_feat, v_feat, residue, rate, w_out, cotangent):
    product_kv = (k_feat.astype(jnp.float32) * v_feat.astype(jnp.float32)).astype(jnp.bfloat16)
    query_ch, mixed_ch = (
        lax.all_to_all(q_feat, "ctx", split_axis=2, concat_axis=1, tiled=True),
        lax.all_to_all(product_kv, "ctx", split_axis=2, concat_axis=1, tiled=True),
    )
    query_ch = query_ch[0]
    mixed_ch = mixed_ch[0]
    length = mixed_ch.shape[0]
    cosine, sine_table, parity = dft_tables(length)
    filt_real, filt_imag, filt_nyq = filter_spectrum(residue, rate, length)
    mix_real, mix_imag, mix_nyq = to_spectrum(cosine, sine_table, parity, mixed_ch)
    conv_out = from_spectrum(
        cosine,
        sine_table,
        parity,
        mix_real * filt_real - mix_imag * filt_imag,
        mix_real * filt_imag + mix_imag * filt_real,
        mix_nyq * filt_nyq,
    )
    gated_out = (query_ch.astype(jnp.float32) * conv_out).astype(jnp.bfloat16)
    w_slab = lax.all_gather(w_out, "fsdp", axis=0, tiled=True)
    token_rows = lax.all_gather(cotangent, "ctx", axis=1, tiled=True)[0]
    grad_rows = jnp.dot(token_rows, w_slab, preferred_element_type=jnp.float32)
    weight_total = jnp.dot(token_rows.T, gated_out, preferred_element_type=jnp.float32)
    grad_gated, weight_total = (grad_rows, weight_total)
    grad_weight = lax.psum_scatter(weight_total, "fsdp", scatter_dimension=0, tiled=True)
    grad_query = (grad_gated * conv_out).astype(jnp.bfloat16)
    grad_conv = (grad_gated * query_ch.astype(jnp.float32)).astype(jnp.bfloat16)
    spec_real, spec_imag, spec_nyq = to_spectrum(cosine, sine_table, parity, grad_conv)
    grad_mix = from_spectrum(
        cosine,
        sine_table,
        parity,
        filt_real * spec_real + filt_imag * spec_imag,
        filt_real * spec_imag - filt_imag * spec_real,
        filt_nyq * spec_nyq,
    ).astype(jnp.bfloat16)
    grad_kernel = from_spectrum(
        cosine,
        sine_table,
        parity,
        mix_real * spec_real + mix_imag * spec_imag,
        mix_real * spec_imag - mix_imag * spec_real,
        mix_nyq * spec_nyq,
    )
    positions = jnp.arange(length).astype(jnp.float32)[:, None, None]
    weighted = grad_kernel[:, :, None] * jnp.exp(-rate[None] * positions)
    resid_term = jnp.sum(weighted, axis=0)
    rate_term = jnp.sum(weighted * positions, axis=0)
    resid_sum, rate_sum = lax.psum((resid_term, rate_term), "fsdp")
    grad_rate = -residue * rate_sum
    back_query, back_mix = (
        lax.all_to_all(grad_query[None], "ctx", split_axis=1, concat_axis=2, tiled=True),
        lax.all_to_all(grad_mix[None], "ctx", split_axis=1, concat_axis=2, tiled=True),
    )
    grad_keys = (back_mix.astype(jnp.float32) * v_feat.astype(jnp.float32)).astype(jnp.bfloat16)
    grad_values = (back_mix.astype(jnp.float32) * k_feat.astype(jnp.float32)).astype(jnp.bfloat16)
    return (back_query, grad_keys, grad_values, grad_weight, resid_sum, grad_rate)


def solution(mesh):
    placed = (
        P("fsdp", "ctx", None),
        P("fsdp", "ctx", None),
        P("fsdp", "ctx", None),
        P("ctx", None),
        P("ctx", None),
        P("fsdp", "ctx"),
        P("fsdp", "ctx", None),
    )
    return jax.shard_map(
        shards,
        mesh=mesh,
        in_specs=placed,
        out_specs=(
            P("fsdp", "ctx", None),
            P("fsdp", "ctx", None),
            P("fsdp", "ctx", None),
            P("fsdp", "ctx"),
            P("ctx", None),
            P("ctx", None),
        ),
        check_vma=False,
    )
```

profile of v0, /device:TPU:3, one launch (start us, length us, event | category | flops | bytes accessed | tf_op | source)
XLA Modules:
  0.0 1089.1 jit_solution(12310339096916643609)
XLA Ops:
  13.9 22.4 %reduce.1 = bf16[4096,128]{1,0:T(8,128)(2,1)S(1)} reduce(bf16[4096,1,128]{2,1,0:T(2,128)(2,1)S(1)} %bitcast.63, bf16[]{:T(256)} %broadcast.159), dimensions={1}, to_apply=%bitcast.37.reduce_sub_computation | reduce | bytes 2097154
  38.0 8.2 all-to-all-start
  46.2 5.0 copy.119
  51.2 23.4 %reduce = bf16[4096,128]{1,0:T(8,128)(2,1)} reduce(bf16[4096,1,128]{2,1,0:T(2,128)(2,1)S(1)} %bitcast.69, bf16[]{:T(256)} %broadcast.159), dimensions={1}, to_apply=%bitcast.41.reduce_sub_computation | reduce | bytes 2097154
  78.8 19.9 %all-to-all-done = bf16[4,2,65536]{2,1,0:T(2,128)(2,1)S(1)} async-done(((bf16[4,2,65536]{2,1,0:T(2,128)(2,1)}), bf16[4,2,65536]{2,1,0:T(2,128)(2,1)S(1)}, u32[]{:S(2)}, u32[]{:S(2)}) %all-to-all-start) | async-done | bytes 1048608 | tf_op jit(solution)/shard_map/all_to_all | solution.py:58
  98.7 4.3 all-to-all-start.2
  103.2 28.7 %fusion.2 = (f32[513,1024]{1,0:T(8,128)}, f32[513,1024]{1,0:T(8,128)S(1)}) fusion(f32[513]{0:T(1024)S(1)} %get-tuple-element.82, f32[1024,16]{0,1:T(8,128)S(1)} %get-tuple-element.75, f32[513]{0:T(1024)S(1)} %get-tuple-element.83, f32[1024,16]{0,1:T(8,128)S(1)} %get-tuple-element.76, f32[1024,16]{0,1:T(8,128)S(1)} %get-tuple-element.74, f32[513]{0:T(1024)S(1)} %fusion.44, ...), kind=kLoop, calls=%fused_computation.4 | loop fusion | flops 125024256 | bytes 4536332 | tf_op jit(solution)/shard_map/reduce_sum | solution.py:29
  131.9 5.0 sine_convert_fusion
  145.5 4.0 reshape.114
  149.5 4.8 bitcast_convert_fusion
  157.5 4.4 fusion.39
  161.9 96.2 %all-gather.5.cloned.1.call-done = bf16[4096,1024]{1,0:T(8,128)(2,1)} async-done(((bf16[64,1024]{1,0:T(8,128)(2,1)}), bf16[4096,1024]{1,0:T(8,128)(2,1)}) %all-gather.5.cloned.1.call-update) | async-done | bytes 8388624 | tf_op jit(solution)/shard_map/all_gather | solution.py:75
  258.1 11.0 %fusion.22 = (bf16[512,1024]{1,0:T(8,128)(2,1)S(1)}, f32[512,1024]{1,0:T(8,128)}) fusion(f32[1,128,4,1024]{3,1,2,0:T(8,128)} %copy.120, bf16[4096,1024]{1,0:T(8,128)(2,1)} %all-gather.5.cloned.1.call-done, bf16[1,512,4096]{2,1,0:T(8,128)(2,1)} %all-gather.3.cloned.1.call-done), kind=kOutput, calls=%fused_computation.35 | convolution fusion | flops 4296015872 | bytes 17825792 | tf_op jit(solution)/shard_map/dot_general | solution.py:77
  278.3 10.1 multiply_reduce_fusion.1
  288.5 5.1 fusion.23
  293.6 8.6 convolution_bitcast_fusion
  302.2 17.5 %copy.125 = f32[4096,1024]{1,0:T(8,128)} copy(f32[4096,1024]{0,1:T(8,128)} %convolution_bitcast_fusion) | data formatting | bytes 33554432
  324.1 6.8 reduce.3
  332.9 6.4 all-to-all-start.3
  342.2 7.8 reduce.2
  353.7 5.9 all-to-all-done.3
  359.6 9.5 all-to-all-start.1
  369.1 406.8 %all-reduce.3.cloned.1.call-done = (f32[1024,16]{0,1:T(8,128)}, f32[1024,16]{0,1:T(8,128)}) async-done(((f32[1024,16]{0,1:T(8,128)}, f32[1024,16]{0,1:T(8,128)}), (f32[1024,16]{0,1:T(8,128)}, f32[1024,16]{0,1:T(8,128)})) %all-reduce.3.cloned.1.call-update) | async-done | bytes 131088 | tf_op jit(solution)/shard_map/psum | solution.py:104
  796.5 285.2 %reduce-scatter.4.cloned.1.call-done = f32[64,1024]{1,0:T(8,128)} async-done(((f32[4096,1024]{1,0:T(8,128)}), f32[64,1024]{1,0:T(8,128)}) %reduce-scatter.4.cloned.1.call-update) | async-done | bytes 262160
  (85 shorter events, 67.9 us)
Async XLA Ops:
  7.2 154.8 %all-gather.3.cloned.1.call-start = ((), (), s32[]{:S(2)}) async-start(), calls=%async_computation.5 | async-start | bytes 5242880 | tf_op jit(solution)/shard_map/all_gather | solution.py:76
  7.9 250.2 %all-gather.5.cloned.1.call-start = ((), (), s32[]{:S(2)}) async-start(), calls=%async_computation.6 | async-start | bytes 8519680 | tf_op jit(solution)/shard_map/all_gather | solution.py:75
  38.0 60.7 %all-to-all-start = ((bf16[4,2,65536]{2,1,0:T(2,128)(2,1)}), bf16[4,2,65536]{2,1,0:T(2,128)(2,1)S(1)}, u32[]{:S(2)}, u32[]{:S(2)}) async-start(bf16[4,2,65536]{2,1,0:T(2,128)(2,1)} %reshape.109), calls=%async_computation | async-start | bytes 2097152 | tf_op jit(solution)/shard_map/all_to_all | solution.py:58
  74.6 3.6 copy-start.15
  74.6 28.6 %copy-start.13 = (f32[1024,16]{0,1:T(8,128)S(1)}, f32[1024,16]{0,1:T(8,128)}, u32[]{:S(2)}) copy-start(f32[1024,16]{0,1:T(8,128)} %param.10) | copy-start | bytes 196612
  98.7 46.8 %all-to-all-start.2 = ((bf16[4,2,65536]{2,1,0:T(2,128)(2,1)}), bf16[4,2,65536]{2,1,0:T(2,128)(2,1)}, u32[]{:S(2)}, u32[]{:S(2)}) async-start(bf16[4,2,65536]{2,1,0:T(2,128)(2,1)} %reshape.113), calls=%async_computation.2 | async-start | bytes 2097152 | tf_op jit(solution)/shard_map/all_to_all | solution.py:57
  103.0 673.0 %all-reduce.3.cloned.1.call-start = ((), (), s32[]{:S(2)}) async-start(), calls=%async_computation.8 | async-start | bytes 262144 | tf_op jit(solution)/shard_map/psum | solution.py:104
  154.3 3.0 copy-start.3
  161.9 107.4 %copy-start.7 = (bf16[512,512]{1,0:T(8,128)(2,1)S(1)}, bf16[512,512]{1,0:T(8,128)(2,1)}, u32[]{:S(2)}) copy-start(bf16[512,512]{1,0:T(8,128)(2,1)} %get-tuple-element.84) | copy-start | bytes 1572868
  161.9 107.4 %copy-start.10 = (bf16[512,512]{1,0:T(8,128)(2,1)S(1)}, bf16[512,512]{1,0:T(8,128)(2,1)}, u32[]{:S(2)}) copy-start(bf16[512,512]{1,0:T(8,128)(2,1)} %get-tuple-element.85) | copy-start | bytes 1572868
  269.4 2.2 copy-start
  271.6 1.6 copy-start.1
  273.2 3.8 copy-start.8
  273.2 3.8 copy-start.11
  277.0 1.3 copy-start.16
  278.3 10.2 copy-start.5
  288.4 793.3 %reduce-scatter.4.cloned.1.call-start = ((), (), s32[]{:S(2)}) async-start(), calls=%async_computation.7 | async-start | bytes 17039360
  288.5 5.2 copy-start.4
  319.7 1.4 copy-start.9
  319.7 1.5 copy-start.12
  332.9 26.7 %all-to-all-start.3 = ((bf16[4,2,65536]{2,1,0:T(2,128)(2,1)}), bf16[4,2,65536]{2,1,0:T(2,128)(2,1)S(1)}, u32[]{:S(2)}, u32[]{:S(2)}) async-start(bf16[4,2,65536]{2,1,0:T(2,128)(2,1)} %reshape.115), calls=%async_computation.3 | async-start | bytes 2097152 | tf_op jit(solution)/shard_map/all_to_all | solution.py:108
  359.6 424.2 %all-to-all-start.1 = ((bf16[4,2,65536]{2,1,0:T(2,128)(2,1)}), bf16[4,2,65536]{2,1,0:T(2,128)(2,1)}, u32[]{:S(2)}, u32[]{:S(2)}) async-start(bf16[4,2,65536]{2,1,0:T(2,128)(2,1)} %reshape.111), calls=%async_computation.1 | async-start | bytes 2097152 | tf_op jit(solution)/shard_map/all_to_all | solution.py:107
  791.0 2.4 copy-start.2
  793.4 288.4 %copy-start.14 = (f32[1024,16]{0,1:T(8,128)S(1)}, f32[1024,16]{0,1:T(8,128)}, u32[]{:S(2)}) copy-start(f32[1024,16]{0,1:T(8,128)} %get-tuple-element.90) | copy-start | bytes 196612
  (1 other events, 1.2 us)
Sparse Core Ops, SparseCore 0:
  9.8 131.7 all-gather.2
  143.5 114.5 all-gather.4
  288.6 487.3 all-reduce.2
  779.1 302.6 reduce-scatter.3
where the time goes:
time: 1110 us; the launch traced here: 1090 us
  waiting for transfers between devices  819 us (74%)
  other arithmetic  121 us (11%)
  local copies, waits for them, and re-layouts  73 us (7%)
  matrix products  33.4 us (3%)
  starting transfers between devices  28.7 us (3%)
  between operations  14.2 us (1%)
    psum x1, waiting for transfers between devices, shards(): resid_sum, rate_sum = lax.psum((resid_term, rate_term), 'fsdp')  407 us
    unnamed x5, waiting for transfers between devices  287 us
    all_gather x1, waiting for transfers between devices, shards(): w_slab = lax.all_gather(w_out, 'fsdp', axis=0, tiled=True)  96.2 us
    unnamed x4, other arithmetic  60.5 us
    unnamed x49, local copies, waits for them, and re-layouts  54.7 us
    reduce_sum x1, other arithmetic, filter_spectrum(): imag_part = -jnp.sum(weights * upward, axis=2)  28.7 us
  transfers between devices with their start and end apart: 8, of which 6 were waited for; matrix products, arithmetic and copies ran while one was open for 18% of the time, Pallas kernels for 0%

commit v1 on v0

v1 whole, which is shorter than its diff:
```python
import jax
import jax.numpy as jnp
from jax import lax
from jax.experimental import pallas as pl
from jax.experimental.pallas import tpu as pltpu
from jax.sharding import PartitionSpec as P

MESH = pl.DeviceIdType.MESH
F32, BF16 = jnp.float32, jnp.bfloat16
TOK = 128
WIDTH = 4096
TILES = 32
MODES = 16
COLS = 512
N_SEND = 96
N_RECV = 112


class Links:
    def __init__(self, send_sems, recv_sems):
        self.send_sems, self.recv_sems = send_sems, recv_sems
        self.sent, self.n_send, self.n_recv = [], 0, 0

    def slot(self, count=1):
        first = self.n_recv
        self.n_recv += count
        assert self.n_recv <= N_RECV
        return first

    def send(self, src, dst, recv, to, only=None):
        sem = self.send_sems.at[self.n_send]
        self.n_send += 1
        assert self.n_send <= N_SEND
        copy = pltpu.make_async_remote_copy(
            src_ref=src, dst_ref=dst, send_sem=sem, recv_sem=self.recv_sems.at[recv],
            device_id=to, device_id_type=MESH)
        if only is None:
            copy.start()
        else:
            pl.when(only)(copy.start)
        self.sent.append((copy, only))

    def local(self, src, dst, recv, only=None):
        copy = pltpu.make_async_copy(src, dst, self.recv_sems.at[recv])
        if only is None:
            copy.start()
        else:
            pl.when(only)(copy.start)

    def wait(self, dst, recv):
        pltpu.make_async_copy(dst, dst, self.recv_sems.at[recv]).wait()

    def finish(self):
        for copy, only in self.sent:
            if only is None:
                copy.wait_send()
            else:
                pl.when(only)(copy.wait_send)


def kernel(q_hbm, k_hbm, v_hbm, par_hbm, w_hbm, cot_hbm,
           gq_hbm, gk_hbm, gv_hbm, gw_hbm, ab_hbm,
           qb, kb, vb, par, cotb, wbuf, xs, cs, gs, es, er, es2, er2, carry, yend,
           gat_send, gat, gsend, grecv, gwp, ra, rb, from_lo, from_hi, vsum,
           zsend, zrecv, fin, gwo, ab, tp_recv, r1, ctx_recv, r2, g_recv, r3, tot,
           gq, gk, gv, send_sems, recv_sems):
    f, zh = lax.axis_index("fsdp"), lax.axis_index("ctx")
    y, zl, x, core = f // 16, (f // 8) % 2, (f // 2) % 4, f % 2
    b, g = f % 8, f // 8
    z = zh * 2 + zl
    links = Links(send_sems, recv_sems)

    def group(delta):
        return (g * 8 + (b + delta) % 8, zh)

    def outer(delta):
        return (((g + delta) % 8) * 8 + b, zh)

    def along_z(delta):
        to = (z + delta) % 8
        return (y * 16 + (to % 2) * 8 + b, to // 2)

    def along_y(delta):
        return (((y + delta) % 4) * 16 + zl * 8 + b, zh)

    def along_x(delta):
        return (g * 8 + ((x + delta) % 4) * 2 + core, zh)

    sibling = (g * 8 + x * 2 + 1 - core, zh)

    def crossed(h):
        return (g * 8 + zh * 2 + h, x)

    barrier = pltpu.get_barrier_semaphore()
    peers = [group(delta) for delta in range(1, 8)] + [along_z(delta) for delta in range(1, 8)]
    for delta in range(1, 4):
        for level in range(2):
            peers.append((((y + delta) % 4) * 16 + level * 8 + b, zh))
    for to in peers:
        pl.semaphore_signal(barrier, inc=1, device_id=to, device_id_type=MESH)

    @pl.when(x != zh)
    def _():
        for h in range(2):
            pl.semaphore_signal(barrier, inc=1, device_id=crossed(h), device_id_type=MESH)
        pl.semaphore_wait(barrier, len(peers) + 2)

    @pl.when(x == zh)
    def _():
        pl.semaphore_wait(barrier, len(peers))

    par_at = links.slot(4)
    for delta in range(1, 4):
        links.send(par_hbm, par.at[zh], par_at + delta, (f, (zh + delta) % 4))
    links.local(par_hbm, par.at[zh], par_at)

    w_at = links.slot(2)
    w_rows = pl.ds(pl.multiple_of(f * 64, 64), 64)
    for h in range(2):
        here = jnp.logical_and(x == zh, core == h)
        src = w_hbm.at[:, pl.ds(h * COLS, COLS)]
        links.send(src, wbuf.at[w_rows, :], w_at + core, crossed(h), only=jnp.logical_not(here))
        links.local(src, wbuf.at[w_rows, :], w_at + core, only=here)

    half = TOK // 2
    x_at = links.slot(4)
    own = cotb.at[b]

    def rows_of(ref, h):
        return ref.at[pl.ds(h * half, half), :]

    for to, h, at in ((1, 0, 0), (-1, 1, 3), (1, 1, 1), (-1, 0, 2)):
        links.send(rows_of(cot_hbm, h), rows_of(own, h), x_at + at, along_x(to))
    cot_at = links.slot(1)
    links.local(cot_hbm, own, cot_at)
    sib_at = links.slot(7)
    links.send(cot_hbm, own, sib_at, sibling)
    load_at = links.slot(3)
    for i, (src, dst) in enumerate(((k_hbm, kb), (v_hbm, vb), (q_hbm, qb))):
        links.local(src, dst, load_at + i)

    links.wait(kb, load_at)
    links.wait(vb, load_at + 1)

    def put(ref, t0, tile, value):
        for i in range(2):
            start = (t0 + 8 * i) * TILES + tile
            ref[pl.ds(start, 8, stride=TILES), :] = value[8 * i:8 * i + 8]

    def get(ref, t0, tile):
        parts = [ref[pl.ds((t0 + 8 * i) * TILES + tile, 8, stride=TILES), :] for i in range(2)]
        return jnp.concatenate(parts, axis=0)

    def each_stripe(body):
        def step(i, _):
            t0 = pl.multiple_of(i * 16, 16)
            for tile in range(TILES):
                body(t0, tile, pl.ds(t0, 16), pl.ds(tile * 128, 128))
            return 0
        lax.fori_loop(0, TOK // 16, step, 0)

    def mix(t0, tile, rows, lanes):
        product = kb[rows, lanes].astype(F32) * vb[rows, lanes].astype(F32)
        put(xs, t0, tile, product.astype(BF16).astype(F32))

    each_stripe(mix)

    for delta in range(1, 4):
        links.wait(par.at[(zh + 4 - delta) % 4], par_at + delta)
    links.wait(par.at[zh], par_at)

    def row_at(t, block):
        return pl.ds(pl.multiple_of(t * TILES + block * 8, 8), 8)

    def each_block(body):
        def step(block, _):
            body(block)
            return 0
        lax.fori_loop(0, 4, step, 0)

    def run_states(src, backward, es):
        def one(block):
            decay = jnp.exp(-par[block, 0:MODES])

            def step(i, state):
                for r in range(8):
                    t = i * 8 + r
                    t = TOK - 1 - t if backward else t
                    state = state * decay + src[row_at(t, block), :][None]
                return state

            state = lax.fori_loop(0, TOK // 8, step, jnp.zeros((MODES, 8, 128), F32))
            es[pl.ds(pl.multiple_of(block * 128, 128), 128), :] = state.reshape(128, 128).astype(BF16)
        each_block(one)

    def exchange_states(sign, es, er):
        at = links.slot(3)
        for delta in range(1, 4):
            to = zh + sign * delta
            ok = to < 4 if sign > 0 else to >= 0
            links.send(es, er.at[delta - 1], at + delta - 1, (f, (to + 4) % 4), only=ok)
        return at

    def gather_states(sign, at, er):
        carry[...] = jnp.zeros(carry.shape, F32)
        for delta in range(1, 4):
            source = zh - sign * delta

            @pl.when(source >= 0 if sign > 0 else source < 4)
            def _():
                links.wait(er.at[delta - 1], at + delta - 1)

                def one(block):
                    rows = pl.ds(pl.multiple_of(block * 128, 128), 128)
                    term = er[delta - 1, rows, :].astype(F32).reshape(MODES, 8, 128)
                    if delta > 1:
                        term = term * jnp.exp(par[block, 0:MODES] * (-float(TOK) * (delta - 1)))
                    carry[block] += term
                each_block(one)

    run_states(xs, False, es)
    s_at = exchange_states(1, es, er)

    links.wait(wbuf.at[pl.ds(0, 64), :], w_at)
    links.wait(wbuf.at[pl.ds(0, 64), :], w_at + 1)

    def slab(zz):
        return pl.ds(pl.multiple_of(y * 1024 + (zz % 2) * 512 + (zz // 2) * 128, 128), 128)

    wz_at = links.slot(7)
    for delta in (1, 7, 2, 6, 3, 5, 4):
        links.send(wbuf.at[slab(z), :], wbuf.at[slab(z), :], wz_at + delta - 1, along_z(delta))

    gather_states(1, s_at, er)

    def tree(v):
        while v.shape[0] > 1:
            n = v.shape[0] // 2
            v = v[:n] + v[n:]
        return v[0]

    def convolve(block):
        decay = jnp.exp(-par[block, 0:MODES])
        weight = par[block, MODES:2 * MODES]

        def step(i, state):
            for r in range(8):
                rows = row_at(i * 8 + r, block)
                state = state * decay + xs[rows, :][None]
                cs[rows, :] = tree(state * weight)
            return state

        yend[block] = lax.fori_loop(0, TOK // 8, step, carry[block])

    each_block(convolve)

    links.wait(qb, load_at + 2)

    def gate(t0, tile, rows, lanes):
        gated = qb[rows, lanes].astype(F32) * get(cs, t0, tile)
        gat_send[tile // 4, rows, pl.ds((tile % 4) * 128, 128)] = gated.astype(BF16)

    each_stripe(gate)

    gat_at = links.slot(8)
    links.local(gat_send.at[b], gat.at[b], gat_at)
    for delta in range(1, 8):
        links.send(gat_send.at[(b + delta) % 8], gat.at[b], gat_at + delta, group(delta))

    left, right, far = ((x + 3) % 4) * 2 + core, ((x + 1) % 4) * 2 + core, ((x + 2) % 4) * 2 + core
    far_at = links.slot(2)
    links.wait(rows_of(cotb.at[left], 0), x_at)
    links.send(rows_of(cotb.at[left], 0), rows_of(cotb.at[left], 0), far_at, along_x(1))
    links.send(rows_of(cotb.at[left], 0), rows_of(cotb.at[left], 0), sib_at + 1, sibling)
    links.wait(rows_of(cotb.at[right], 1), x_at + 3)
    links.send(rows_of(cotb.at[right], 1), rows_of(cotb.at[right], 1), far_at + 1, along_x(-1))
    links.send(rows_of(cotb.at[right], 1), rows_of(cotb.at[right], 1), sib_at + 2, sibling)
    links.wait(rows_of(cotb.at[left], 1), x_at + 1)
    links.send(rows_of(cotb.at[left], 1), rows_of(cotb.at[left], 1), sib_at + 3, sibling)
    links.wait(rows_of(cotb.at[right], 0), x_at + 2)
    links.send(rows_of(cotb.at[right], 0), rows_of(cotb.at[right], 0), sib_at + 4, sibling)

    for delta in range(1, 8):
        links.wait(wbuf.at[slab((z + 8 - delta) % 8), :], wz_at + delta - 1)

    def w_half(yy, h):
        return wbuf.at[pl.ds(pl.multiple_of(((yy + 4) % 4) * 1024 + h * 512, 512), 512), :]

    wy_at = links.slot(4)
    for to, h, at in ((1, 0, 0), (-1, 1, 3), (1, 1, 1), (-1, 0, 2)):
        links.send(w_half(y, h), w_half(y, h), wy_at + at, along_y(to))

    for h in range(2):
        links.wait(rows_of(cotb.at[far], h), far_at + h)
        links.send(rows_of(cotb.at[far], h), rows_of(cotb.at[far], h), sib_at + 5 + h, sibling)

    wf_at = links.slot(2)
    links.wait(w_half(y - 1, 0), wy_at)
    links.send(w_half(y - 1, 0), w_half(y - 1, 0), wf_at, along_y(1))
    links.wait(w_half(y + 1, 1), wy_at + 3)
    links.send(w_half(y + 1, 1), w_half(y + 1, 1), wf_at + 1, along_y(-1))

    links.wait(own, cot_at)
    other = 1 - 2 * core
    links.wait(cotb.at[b + other], sib_at)
    links.wait(rows_of(cotb.at[left + other], 0), sib_at + 1)
    links.wait(rows_of(cotb.at[right + other], 1), sib_at + 2)
    links.wait(rows_of(cotb.at[left + other], 1), sib_at + 3)
    links.wait(rows_of(cotb.at[right + other], 0), sib_at + 4)
    for h in range(2):
        links.wait(rows_of(cotb.at[far + other], h), sib_at + 5 + h)
    for delta in range(8):
        links.wait(gat.at[(b + 8 - delta) % 8], gat_at + delta)

    def part_rows(delta):
        return pl.multiple_of(((y + delta + 4) % 4) * 1024, 1024)

    def weight_part(delta, dst, base):
        def step(i, _):
            at = pl.multiple_of(part_rows(delta) + i * 256, 256)
            lhs = cotb[:, :, pl.ds(at, 256)].reshape(8 * TOK, 256)
            out = lax.dot_general(lhs, gat[...].reshape(8 * TOK, COLS), (((0,), (0,)), ((), ())),
                                  preferred_element_type=F32)
            dst[pl.ds(pl.multiple_of(base + i * 256, 256), 256), :] = out.astype(dst.dtype)
            return 0
        lax.fori_loop(0, 4, step, 0)

    def part_half(delta, h):
        return gwp.at[pl.ds(pl.multiple_of(part_rows(delta) + h * 512, 512), 512), :]

    def half_of(ref, h):
        return ref.at[pl.ds(h * 512, 512), :]

    gy_at = links.slot(6)
    weight_part(2, gwp, part_rows(2))
    links.send(part_half(2, 0), ra, gy_at, along_y(1))
    links.send(part_half(2, 1), rb, gy_at + 1, along_y(-1))
    weight_part(1, gwp, part_rows(1))
    links.send(part_half(1, 1), half_of(from_lo, 1), gy_at + 2, along_y(1))
    weight_part(-1, gwp, part_rows(-1))
    links.send(part_half(-1, 0), half_of(from_hi, 0), gy_at + 3, along_y(-1))
    weight_part(0, vsum, 0)

    links.wait(w_half(y - 1, 1), wy_at + 1)
    links.wait(w_half(y + 1, 0), wy_at + 2)
    links.wait(w_half(y + 2, 0), wf_at)
    links.wait(w_half(y + 2, 1), wf_at + 1)

    def project(i, _):
        total = jnp.zeros((2 * TOK, COLS), F32)
        for part in range(4):
            lhs = cotb[pl.ds(i * 2, 2), :, pl.ds(part * 1024, 1024)].reshape(2 * TOK, 1024)
            total += jnp.dot(lhs, wbuf[pl.ds(part * 1024, 1024), :], preferred_element_type=F32)
        gsend[pl.ds(i * 2, 2)] = total.astype(BF16).reshape(2, TOK, COLS)
        return 0

    lax.fori_loop(0, 4, project, 0)
    g_at = links.slot(8)
    links.local(gsend.at[b], grecv.at[b], g_at)
    for delta in range(1, 8):
        links.send(gsend.at[(b + delta) % 8], grecv.at[b], g_at + delta, group(delta))

    def add_half(delta, h, term):
        def step(i, _):
            rows = pl.ds(pl.multiple_of(part_rows(delta) + h * 512 + i * 64, 64), 64)
            theirs = term[pl.ds(pl.multiple_of(i * 64, 64), 64), :].astype(F32)
            gwp[rows, :] = (gwp[rows, :].astype(F32) + theirs).astype(BF16)
            return 0
        lax.fori_loop(0, 8, step, 0)

    links.wait(ra, gy_at)
    add_half(1, 0, ra)
    links.send(part_half(1, 0), half_of(from_lo, 0), gy_at + 4, along_y(1))
    links.wait(rb, gy_at + 1)
    add_half(-1, 1, rb)
    links.send(part_half(-1, 1), half_of(from_hi, 1), gy_at + 5, along_y(-1))

    for delta in range(8):
        links.wait(grecv.at[(b + 8 - delta) % 8], g_at + delta)

    def grad_gate(t0, tile, rows, lanes):
        grad = grecv[tile // 4, rows, pl.ds((tile % 4) * 128, 128)].astype(F32)
        gq[rows, lanes] = (grad * get(cs, t0, tile)).astype(BF16)
        put(gs, t0, tile, (grad * qb[rows, lanes].astype(F32)).astype(BF16).astype(F32))

    each_stripe(grad_gate)
    out_at = links.slot(3)
    links.local(gq, gq_hbm, out_at)

    run_states(gs, True, es2)
    t_at = exchange_states(-1, es2, er2)

    links.wait(half_of(from_lo, 1), gy_at + 2)
    links.wait(half_of(from_lo, 0), gy_at + 4)
    links.wait(half_of(from_hi, 0), gy_at + 3)
    links.wait(half_of(from_hi, 1), gy_at + 5)

    def add_y(i, _):
        rows = pl.ds(pl.multiple_of(i * 64, 64), 64)
        vsum[rows, :] += from_lo[rows, :].astype(F32) + from_hi[rows, :].astype(F32)
        return 0

    lax.fori_loop(0, 16, add_y, 0)

    def z_rows(zz):
        return pl.ds(pl.multiple_of((zz % 2) * 512 + (zz // 2) * 128, 128), 128)

    gz_at = links.slot(7)
    for delta in (4, 3, 5, 2, 6, 1, 7):
        zsend[delta - 1] = vsum[z_rows((z + delta) % 8), :].astype(BF16)
        links.send(zsend.at[delta - 1], zrecv.at[delta - 1], gz_at + delta - 1, along_z(delta))

    gather_states(-1, t_at, er2)

    part = 4

    def adjoint(block):
        for m in range(0, MODES, part):
            rate = par[block, m:m + part]
            decay, growth = jnp.exp(-rate), jnp.exp(rate)
            weight = par[block, MODES + m:MODES + m + part]

            def step(i, carried):
                p, s, da, db = carried
                for r in range(8):
                    rows = row_at(TOK - 1 - (i * 8 + r), block)
                    xt = xs[rows, :][None]
                    p = p * decay + gs[rows, :][None]
                    da = da + p * xt
                    s = (s - xt) * growth
                    db = db + p * s
                    out = tree(p * weight)
                    if m:
                        out = out + cs[rows, :]
                    cs[rows, :] = out
                return p, s, da, db

            zero = jnp.zeros((part, 8, 128), F32)
            start = (carry[block, m:m + part], yend[block, m:m + part], zero, zero)
            _, _, da, db = lax.fori_loop(0, TOK // 8, step, start)
            ab[block, m:m + part] = da
            ab[block, MODES + m:MODES + m + part] = db * decay

    each_block(adjoint)

    tp_at = links.slot(7)
    for delta in range(1, 8):
        to = pl.ds(((b + delta) % 8) * 4, 4)
        links.send(ab.at[:, to], tp_recv.at[delta - 1], tp_at + delta - 1, group(delta))

    def grads(t0, tile, rows, lanes):
        grad = get(cs, t0, tile).astype(BF16).astype(F32)
        gk[rows, lanes] = (grad * vb[rows, lanes].astype(F32)).astype(BF16)
        gv[rows, lanes] = (grad * kb[rows, lanes].astype(F32)).astype(BF16)

    each_stripe(grads)
    links.local(gk, gk_hbm, out_at + 1)
    links.local(gv, gv_hbm, out_at + 2)

    r1[...] = ab[:, pl.ds(b * 4, 4)]
    for delta in range(1, 8):
        links.wait(tp_recv.at[delta - 1], tp_at + delta - 1)
        r1[...] += tp_recv[delta - 1]
    c_at = links.slot(3)
    for delta in range(1, 4):
        links.send(r1.at[(zh + delta) % 4], ctx_recv.at[delta - 1], c_at + delta - 1, (f, (zh + delta) % 4))

    fin[...] = vsum[z_rows(z), :]
    for delta in range(1, 8):
        links.wait(zrecv.at[delta - 1], gz_at + delta - 1)
        fin[...] += zrecv[delta - 1].astype(F32)
    fin_at = links.slot(2)
    for h in range(2):
        here = jnp.logical_and(x == zh, core == h)
        src = fin.at[pl.ds(h * 64, 64), :]
        links.send(src, gwo.at[core], fin_at + core, crossed(h), only=jnp.logical_not(here))
        links.local(src, gwo.at[core], fin_at + core, only=here)

    r2[...] = r1[zh]
    for delta in range(1, 4):
        links.wait(ctx_recv.at[delta - 1], c_at + delta - 1)
        r2[...] += ctx_recv[delta - 1]
    o_at = links.slot(7)
    for delta in range(1, 8):
        links.send(r2, g_recv.at[delta - 1], o_at + delta - 1, outer(delta))

    gwo_at = links.slot(2)
    for h in range(2):
        links.wait(gwo.at[h], fin_at + h)
        links.local(gwo.at[h], gw_hbm.at[:, pl.ds(h * COLS, COLS)], gwo_at + h)

    for delta in range(1, 8):
        links.wait(g_recv.at[delta - 1], o_at + delta - 1)
    total = jnp.zeros((4, 8, 128), F32)
    for source in range(8):
        delta = (g + 8 - source) % 8
        theirs = g_recv[jnp.maximum(delta - 1, 0)]
        total = total + jnp.where(delta == 0, r2[...], theirs)
    r3[...] = total
    e_at = links.slot(8)
    for delta in range(1, 8):
        links.send(r3, tot.at[pl.ds(b * 4, 4)], e_at + delta, group(delta))
    links.local(r3, tot.at[pl.ds(b * 4, 4)], e_at)
    for delta in range(8):
        links.wait(tot.at[pl.ds(((b + 8 - delta) % 8) * 4, 4)], e_at + delta)
    ab_at = links.slot(1)
    links.local(tot, ab_hbm, ab_at)

    links.wait(gq, out_at)
    links.wait(gk, out_at + 1)
    links.wait(gv, out_at + 2)
    for h in range(2):
        links.wait(gwo.at[h], gwo_at + h)
    links.wait(tot, ab_at)
    links.finish()


def shards(q_feat, k_feat, v_feat, residue, rate, w_out, cotangent):
    params = jnp.concatenate([rate.T, residue.T], axis=0).reshape(2 * MODES, 8, 128)
    anyspace = pl.BlockSpec(memory_space=pl.ANY)
    flat = (TOK, WIDTH)
    act = jax.ShapeDtypeStruct(flat, BF16)
    v = pltpu.VMEM
    grad_q, grad_k, grad_v, grad_weight, sums = pl.pallas_call(
        kernel,
        out_shape=(act, act, act, jax.ShapeDtypeStruct((64, 1024), F32),
                   jax.ShapeDtypeStruct((2 * MODES, 8, 128), F32)),
        in_specs=[anyspace] * 6,
        out_specs=[anyspace] * 5,
        scratch_shapes=[
            v(flat, BF16), v(flat, BF16), v(flat, BF16),
            v((4, 2 * MODES, 8, 128), F32),
            v((8, TOK, WIDTH), BF16), v((WIDTH, COLS), BF16),
            v((WIDTH, 128), F32), v((WIDTH, 128), F32), v((WIDTH, 128), F32),
            v((512, 128), BF16), v((3, 512, 128), BF16),
            v((512, 128), BF16), v((3, 512, 128), BF16),
            v((4, MODES, 8, 128), F32), v((4, MODES, 8, 128), F32),
            v((8, TOK, COLS), BF16), v((8, TOK, COLS), BF16),
            v((8, TOK, COLS), BF16), v((8, TOK, COLS), BF16),
            v((WIDTH, COLS), BF16),
            v((512, COLS), BF16), v((512, COLS), BF16),
            v((1024, COLS), BF16), v((1024, COLS), BF16),
            v((1024, COLS), F32),
            v((7, 128, COLS), BF16), v((7, 128, COLS), BF16),
            v((128, COLS), F32), v((2, 64, COLS), F32),
            v((4, 2 * MODES, 8, 128), F32),
            v((7, 4, 4, 8, 128), F32), v((4, 4, 8, 128), F32),
            v((3, 4, 8, 128), F32), v((4, 8, 128), F32),
            v((7, 4, 8, 128), F32), v((4, 8, 128), F32),
            v((2 * MODES, 8, 128), F32),
            v(flat, BF16), v(flat, BF16), v(flat, BF16),
            pltpu.SemaphoreType.DMA((N_SEND,)),
            pltpu.SemaphoreType.DMA((N_RECV,)),
        ],
        compiler_params=pltpu.CompilerParams(
            collective_id=0, has_side_effects=True, vmem_limit_bytes=60 * 1024 * 1024),
    )(q_feat[0], k_feat[0], v_feat[0], params, w_out, cotangent[0])
    sums = sums.reshape(2, MODES, 1024)
    grad_residue = sums[0].T
    grad_rate = -residue * sums[1].T
    return grad_q[None], grad_k[None], grad_v[None], grad_weight, grad_residue, grad_rate


def solution(mesh):
    act, modes, proj = P("fsdp", "ctx", None), P("ctx", None), P("fsdp", "ctx")
    return jax.shard_map(
        shards,
        mesh=mesh,
        in_specs=(act, act, act, modes, modes, proj, act),
        out_specs=(act, act, act, proj, modes, modes),
        check_vma=False,
    )
```

time: 1110 us -> 195 us (0.18); the launches traced: 1090 us -> 191 us
  waiting for transfers between devices: 819 us -> 0 us
  Pallas kernels: 0 us -> 181 us
  other arithmetic: 121 us -> 1.53 us
  local copies, waits for them, and re-layouts: 73 us -> 8.02 us
  matrix products: 33.4 us -> 0 us
  starting transfers between devices: 28.7 us -> 0 us
  between operations: 14.2 us -> 0.67 us
    psum x1 -> x0, waiting for transfers between devices: 407 us -> none  [shards(): resid_sum, rate_sum = lax.psum((resid_term, rate_term), 'fsdp')]
    unnamed x5 -> x0, waiting for transfers between devices: 287 us -> none
    pallas_call x0 -> x1, Pallas kernels: none -> 181 us  [shards(): pl.pallas_call(kernel, out_shape=(act, act, act, jax.ShapeDtypeStruct((64...]
    all_gather x2 -> x0, waiting for transfers between devices: 96.2 us -> none  [the longest x1 96.2 us: shards(): w_slab = lax.all_gather(w_out, 'fsdp', axis=0, tiled=True)]
    unnamed x4 -> x1, other arithmetic: 60.5 us -> 0.88 us
    unnamed x49 -> x14, local copies, waits for them, and re-layouts: 54.7 us -> 7.1 us
    reduce_sum x2 -> x0, other arithmetic: 38.8 us -> none  [the longest x1 28.7 us: filter_spectrum(): imag_part = -jnp.sum(weights * upward, axis=2)]
    dot_general x9 -> x0, matrix products: 33.4 us -> none  [the longest x1 11 us: shards(): grad_rows = jnp.dot(token_rows, w_slab, preferred_element_type=jnp.float32)]
  transfers between devices with their start and end apart: 8 -> 0, of which waited for: 6 -> 0; matrix products, arithmetic and copies ran while one was open for 18% -> 0% of each run, Pallas kernels for 0% -> 0%
where the time goes in v1:
time: 195 us; the launch traced here: 191 us
  Pallas kernels  181 us (93%)
  local copies, waits for them, and re-layouts  8.02 us (4%)
    pallas_call x1, Pallas kernels, shards(): pl.pallas_call(kernel, out_shape=(act, act, act, jax.ShapeDtypeStruct((64...  181 us
    unnamed x14, local copies, waits for them, and re-layouts  7.1 us

profile of v1, /device:TPU:3, one launch (start us, length us, event | category | flops | bytes accessed | tf_op | source)
XLA Modules:
  0.0 191.2 jit_solution(7999328520089172465)
XLA Ops:
  0.6 0.9 maximum_bitcast_fusion
  1.5 0.7 copy.13
  2.2 181.0 %shard_map.118 = (bf16[128,4096]{1,0:T(8,128)(2,1)}, bf16[128,4096]{1,0:T(8,128)(2,1)}, bf16[128,4096]{1,0:T(8,128)(2,1)}, f32[64,1024]{1,0:T(8,128)}, f32[32,8,128]{2,1,0:T(8,128)}) custom-call(bf16[128,4096]{1,0:T(8,128)(2,1)} %bitcast.28, bf16[128,4096]{1,0:T(8,128)(2,1)} %bitcast.29, bf16[128,4096]{1,0:T(8,128)(2,1)} %bitcast.30, ...), custom_call_target="tpu_custom_call" | custom-call | tf_op jit(solution)/shard_map/pallas_call | solution.py:524
  183.2 0.0 copy-start.3
  183.2 0.9 fusion.1
  184.1 0.0 copy-done.3
  184.1 0.6 fusion
  184.8 0.6 copy.18
  185.4 0.0 copy-start.1
  185.4 2.4 %copy.23 = bf16[1,128,4096]{2,1,0:T(8,128)(2,1)} copy(bf16[1,128,4096]{2,1,0:T(8,128)(2,1)} %bitcast.34) | data formatting | bytes 2097152
  187.8 0.0 copy-done.1
  187.8 0.0 copy-start
  187.8 1.0 copy.24
  188.8 0.6 copy-done
  189.4 0.0 copy-start.2
  189.4 1.0 copy.25
  190.4 0.1 copy-done.2
  190.5 0.7 copy.26
Async XLA Ops:
  183.2 0.9 copy-start.3
  185.4 2.4 %copy-start.1 = (bf16[128,4096]{1,0:T(8,128)(2,1)S(1)}, bf16[128,4096]{1,0:T(8,128)(2,1)}, u32[]{:S(2)}) copy-start(bf16[128,4096]{1,0:T(8,128)(2,1)} %get-tuple-element.12) | copy-start | bytes 3145732
  187.8 1.6 copy-start
  189.4 1.1 copy-start.2

commit v2 on v1

v2 whole, which is shorter than its diff:
```python
import jax
import jax.numpy as jnp
from jax import lax
from jax.experimental import pallas as pl
from jax.experimental.pallas import tpu as pltpu
from jax.sharding import PartitionSpec as P

MESH = pl.DeviceIdType.MESH
F32, BF16 = jnp.float32, jnp.bfloat16
TOK = 128
WIDTH = 4096
TILES = 32
MODES = 16
COLS = 512
N_SEND = 256
N_RECV = 256


class Links:
    def __init__(self, send_sems, recv_sems):
        self.send_sems, self.recv_sems = send_sems, recv_sems
        self.sent, self.n_send, self.n_recv = [], 0, 0

    def slot(self, count=1):
        first = self.n_recv
        self.n_recv += count
        assert self.n_recv <= N_RECV
        return first

    def send(self, src, dst, recv, to, only=None):
        sem = self.send_sems.at[self.n_send]
        self.n_send += 1
        assert self.n_send <= N_SEND
        copy = pltpu.make_async_remote_copy(
            src_ref=src, dst_ref=dst, send_sem=sem, recv_sem=self.recv_sems.at[recv],
            device_id=to, device_id_type=MESH)
        if only is None:
            copy.start()
        else:
            pl.when(only)(copy.start)
        self.sent.append((copy, only))

    def local(self, src, dst, recv, only=None):
        copy = pltpu.make_async_copy(src, dst, self.recv_sems.at[recv])
        if only is None:
            copy.start()
        else:
            pl.when(only)(copy.start)

    def wait(self, dst, recv):
        pltpu.make_async_copy(dst, dst, self.recv_sems.at[recv]).wait()

    def finish(self):
        for copy, only in self.sent:
            if only is None:
                copy.wait_send()
            else:
                pl.when(only)(copy.wait_send)


def kernel(q_hbm, k_hbm, v_hbm, par_hbm, w_hbm, cot_hbm,
           gq_hbm, gk_hbm, gv_hbm, gw_hbm, ab_hbm,
           qb, kb, vb, par, cotb, wbuf, xs, cs, gs, es, er, es2, er2, carry, yend,
           gat_send, gat, gsend, grecv, gwp, ra, rb, from_lo, from_hi, vsum,
           zsend, zrecv, fin, gwo, ab, tp_recv, r1, ctx_recv, r2, g_recv, r3, tot,
           gq, gk, gv, send_sems, recv_sems):
    f, zh = lax.axis_index("fsdp"), lax.axis_index("ctx")
    y, zl, x, core = f // 16, (f // 8) % 2, (f // 2) % 4, f % 2
    b, g = f % 8, f // 8
    z = zh * 2 + zl
    links = Links(send_sems, recv_sems)

    def group(delta):
        return (g * 8 + (b + delta) % 8, zh)

    def outer(delta):
        return (((g + delta) % 8) * 8 + b, zh)

    def along_z(delta):
        to = (z + delta) % 8
        return (y * 16 + (to % 2) * 8 + b, to // 2)

    def along_y(delta):
        return (((y + delta) % 4) * 16 + zl * 8 + b, zh)

    def along_x(delta):
        return (g * 8 + ((x + delta) % 4) * 2 + core, zh)

    sibling = (g * 8 + x * 2 + 1 - core, zh)

    def crossed(h):
        return (g * 8 + zh * 2 + h, x)

    barrier = pltpu.get_barrier_semaphore()
    peers = [group(delta) for delta in range(1, 8)] + [along_z(delta) for delta in range(1, 8)]
    for delta in range(1, 4):
        for level in range(2):
            peers.append((((y + delta) % 4) * 16 + level * 8 + b, zh))
    for to in peers:
        pl.semaphore_signal(barrier, inc=1, device_id=to, device_id_type=MESH)

    @pl.when(x != zh)
    def _():
        for h in range(2):
            pl.semaphore_signal(barrier, inc=1, device_id=crossed(h), device_id_type=MESH)

    load_at = links.slot(3)
    for i, (src, dst) in enumerate(((k_hbm, kb), (v_hbm, vb), (q_hbm, qb))):
        links.local(src, dst, load_at + i)
    own = cotb.at[b]
    cot_at = links.slot(1)
    links.local(cot_hbm, own, cot_at)
    own_par_at = links.slot(1)
    links.local(par_hbm, par.at[zh], own_par_at)

    links.wait(kb, load_at)
    links.wait(vb, load_at + 1)

    def put(ref, t0, tile, value):
        for i in range(2):
            start = (t0 + 8 * i) * TILES + tile
            ref[pl.ds(start, 8, stride=TILES), :] = value[8 * i:8 * i + 8]

    def get(ref, t0, tile):
        parts = [ref[pl.ds((t0 + 8 * i) * TILES + tile, 8, stride=TILES), :] for i in range(2)]
        return jnp.concatenate(parts, axis=0)

    def each_tile(body, block):
        def step(i, _):
            t0 = pl.multiple_of(i * 16, 16)
            for k in range(8):
                lanes = pl.ds(pl.multiple_of(block * 1024 + k * 128, 128), 128)
                body(t0, block * 8 + k, k, pl.ds(t0, 16), lanes)
            return 0
        lax.fori_loop(0, TOK // 16, step, 0)

    def each_block(body):
        def step(block, _):
            body(block)
            return 0
        lax.fori_loop(0, 4, step, 0)

    def mix(t0, tile, k, rows, lanes):
        product = kb[rows, lanes].astype(F32) * vb[rows, lanes].astype(F32)
        put(xs, t0, tile, product.astype(BF16).astype(F32))

    each_block(lambda block: each_tile(mix, block))

    @pl.when(x != zh)
    def _():
        pl.semaphore_wait(barrier, len(peers) + 2)

    @pl.when(x == zh)
    def _():
        pl.semaphore_wait(barrier, len(peers))

    par_at = links.slot(3)
    sib_par_at = links.slot(3)

    def par_half(j, c):
        return par.at[j, pl.ds(c * MODES, MODES)]

    w_at = links.slot(2)
    w_rows = pl.ds(pl.multiple_of(f * 64, 64), 64)
    for h in range(2):
        here = jnp.logical_and(x == zh, core == h)
        src = w_hbm.at[:, pl.ds(h * COLS, COLS)]
        links.send(src, wbuf.at[w_rows, :], w_at + core, crossed(h), only=jnp.logical_not(here))
        links.local(src, wbuf.at[w_rows, :], w_at + core, only=here)
    for delta in range(1, 4):
        links.send(par_hbm.at[pl.ds(core * MODES, MODES)], par_half(zh, core), par_at + delta - 1,
                   (f, (zh + delta) % 4))

    half = TOK // 2
    x_at = links.slot(4)

    def rows_of(ref, h):
        return ref.at[pl.ds(h * half, half), :]

    def send_x(to, h, at):
        links.send(rows_of(cot_hbm, h), rows_of(own, h), x_at + at, along_x(to))

    send_x(1, 0, 0)
    send_x(-1, 1, 3)
    sib_at = links.slot(7)

    links.wait(wbuf.at[pl.ds(0, 64), :], w_at)
    links.wait(wbuf.at[pl.ds(0, 64), :], w_at + 1)

    def w_block(dy, dz, h=None):
        zz = (z + dz + 8) % 8
        start = ((y + dy + 4) % 4) * 1024 + (zz % 2) * 512 + (zz // 2) * 128
        if h is None:
            return wbuf.at[pl.ds(pl.multiple_of(start, 128), 128), :]
        return wbuf.at[pl.ds(pl.multiple_of(start + h * 64, 64), 64), :]

    up_at = links.slot(5)
    down_at = links.slot(5)
    wy_at = links.slot(8 * 6)

    def pass_z(step):
        for to, at in ((1, up_at), (-1, down_at)):
            ref = w_block(0, -to * step, None if step < 3 else (1 - to) // 2)
            links.send(ref, ref, at + step, along_z(to))

    def wait_z(step):
        for to, at in ((1, up_at), (-1, down_at)):
            links.wait(w_block(0, -to * step, None if step < 4 else (1 - to) // 2), at + step - 1)

    def send_y(dz):
        base = wy_at + (dz + 8) % 8 * 6
        for to, h, at in ((1, 0, 0), (-1, 1, 1), (1, 1, 2), (-1, 0, 3)):
            links.send(w_block(0, dz, h), w_block(0, dz, h), base + at, along_y(to))

    def pass_y(dz):
        base = wy_at + (dz + 8) % 8 * 6
        links.wait(w_block(-1, dz, 0), base)
        links.send(w_block(-1, dz, 0), w_block(-1, dz, 0), base + 4, along_y(1))
        links.wait(w_block(1, dz, 1), base + 1)
        links.send(w_block(1, dz, 1), w_block(1, dz, 1), base + 5, along_y(-1))

    def wait_y(dz):
        base = wy_at + (dz + 8) % 8 * 6
        links.wait(w_block(-1, dz, 1), base + 2)
        links.wait(w_block(1, dz, 0), base + 3)
        links.wait(w_block(2, dz, 0), base + 4)
        links.wait(w_block(2, dz, 1), base + 5)

    pass_z(0)
    send_y(0)
    send_x(1, 1, 1)
    send_x(-1, 0, 2)
    links.send(cot_hbm, own, sib_at, sibling)

    for delta in range(1, 4):
        source = (zh + 4 - delta) % 4
        links.wait(par_half(source, core), par_at + delta - 1)
        links.send(par_half(source, core), par_half(source, core), sib_par_at + delta - 1, sibling)
    for delta in range(1, 4):
        links.wait(par_half((zh + 4 - delta) % 4, 1 - core), sib_par_at + delta - 1)
    links.wait(par.at[zh], own_par_at)

    def row_at(t, block):
        return pl.ds(pl.multiple_of(t * TILES + block * 8, 8), 8)

    def state_rows(block):
        return pl.ds(pl.multiple_of(block * 128, 128), 128)

    def run_states(src, backward, es, block):
        decay = jnp.exp(-par[block, 0:MODES])

        def step(i, state):
            for r in range(8):
                t = i * 8 + r
                t = TOK - 1 - t if backward else t
                state = state * decay + src[row_at(t, block), :][None]
            return state

        state = lax.fori_loop(0, TOK // 8, step, jnp.zeros((MODES, 8, 128), F32))
        es[state_rows(block), :] = state.reshape(128, 128).astype(BF16)

    def send_states(sign, es, er, at, block, turn):
        for delta in range(1, 4):
            to = zh + sign * delta
            ok = to < 4 if sign > 0 else to >= 0
            links.send(es.at[state_rows(block), :], er.at[delta - 1, state_rows(block), :],
                       at + turn * 3 + delta - 1, (f, (to + 4) % 4), only=ok)

    def gather_states(sign, er, at, block, turn):
        carry[block] = jnp.zeros((MODES, 8, 128), F32)
        for delta in range(1, 4):
            source = zh - sign * delta

            @pl.when(source >= 0 if sign > 0 else source < 4)
            def _():
                links.wait(er.at[delta - 1, state_rows(block), :], at + turn * 3 + delta - 1)
                term = er[delta - 1, state_rows(block), :].astype(F32).reshape(MODES, 8, 128)
                if delta > 1:
                    term = term * jnp.exp(par[block, 0:MODES] * (-float(TOK) * (delta - 1)))
                carry[block] += term

    s_at = links.slot(12)
    for block in range(4):
        run_states(xs, False, es, block)
        send_states(1, es, er, s_at, block, block)

    wait_z(1)
    pass_z(1)
    send_y(-1)
    send_y(1)
    pass_y(0)

    left, right, far = ((x + 3) % 4) * 2 + core, ((x + 1) % 4) * 2 + core, ((x + 2) % 4) * 2 + core
    far_at = links.slot(2)

    def share(slot, h, at):
        ref = rows_of(cotb.at[slot], h)
        links.send(ref, ref, sib_at + at, sibling)

    links.wait(rows_of(cotb.at[left], 0), x_at)
    links.send(rows_of(cotb.at[left], 0), rows_of(cotb.at[left], 0), far_at, along_x(1))
    links.wait(rows_of(cotb.at[right], 1), x_at + 3)
    links.send(rows_of(cotb.at[right], 1), rows_of(cotb.at[right], 1), far_at + 1, along_x(-1))
    share(left, 0, 1)
    share(right, 1, 2)

    wait_z(2)
    pass_z(2)
    send_y(-2)
    send_y(2)
    pass_y(-1)
    pass_y(1)

    def tree(v):
        while v.shape[0] > 1:
            n = v.shape[0] // 2
            v = v[:n] + v[n:]
        return v[0]

    def convolve(block):
        decay = jnp.exp(-par[block, 0:MODES])
        weight = par[block, MODES:2 * MODES]

        def step(i, state):
            for r in range(8):
                rows = row_at(i * 8 + r, block)
                state = state * decay + xs[rows, :][None]
                cs[rows, :] = tree(state * weight)
            return state

        yend[block] = lax.fori_loop(0, TOK // 8, step, carry[block])

    def gate(t0, tile, k, rows, lanes):
        gated = qb[rows, lanes].astype(F32) * get(cs, t0, tile)
        gat_send[tile // 4, rows, pl.ds((k % 4) * 128, 128)] = gated.astype(BF16)

    links.wait(qb, load_at + 2)
    for block in range(4):
        gather_states(1, er, s_at, block, block)
        convolve(block)
        each_tile(gate, block)

    wait_z(3)
    pass_z(3)
    send_y(-3)
    send_y(3)
    pass_y(-2)
    pass_y(2)

    wait_z(4)
    send_y(4)
    pass_y(-3)
    pass_y(3)
    links.wait(rows_of(cotb.at[left], 1), x_at + 1)
    share(left, 1, 3)
    links.wait(rows_of(cotb.at[right], 0), x_at + 2)
    share(right, 0, 4)
    pass_y(4)
    for h in range(2):
        links.wait(rows_of(cotb.at[far], h), far_at + h)
        share(far, h, 5 + h)
    gat_at = links.slot(8)
    links.local(gat_send.at[b], gat.at[b], gat_at)
    for delta in range(1, 8):
        links.send(gat_send.at[(b + delta) % 8], gat.at[b], gat_at + delta, group(delta))
    for dz in range(8):
        wait_y(dz)

    other = 1 - 2 * core
    g_at = links.slot(8)

    def project(chip):
        total = jnp.zeros((2 * TOK, COLS), F32)
        for part in range(4):
            lhs = cotb[pl.ds(chip * 2, 2), :, pl.ds(part * 1024, 1024)].reshape(2 * TOK, 1024)
            total += jnp.dot(lhs, wbuf[pl.ds(part * 1024, 1024), :], preferred_element_type=F32)
        gsend[pl.ds(chip * 2, 2)] = total.astype(BF16).reshape(2, TOK, COLS)

    def return_chip(dx):
        chip = (x + dx) % 4
        for dc in range(2):
            to = chip * 2 + (core + dc) % 2
            if dx == 0 and dc == 0:
                links.local(gsend.at[b], grecv.at[b], g_at + b)
            else:
                links.send(gsend.at[to], grecv.at[b], g_at + b, (g * 8 + to, zh))

    links.wait(own, cot_at)
    links.wait(cotb.at[b + other], sib_at)
    project(x)
    return_chip(0)
    links.wait(rows_of(cotb.at[left + other], 0), sib_at + 1)
    links.wait(rows_of(cotb.at[left + other], 1), sib_at + 3)
    project((x + 3) % 4)
    return_chip(3)
    links.wait(rows_of(cotb.at[right + other], 1), sib_at + 2)
    links.wait(rows_of(cotb.at[right + other], 0), sib_at + 4)
    project((x + 1) % 4)
    return_chip(1)
    for h in range(2):
        links.wait(rows_of(cotb.at[far + other], h), sib_at + 5 + h)
    project((x + 2) % 4)
    return_chip(2)

    for delta in range(8):
        links.wait(gat.at[(b + 8 - delta) % 8], gat_at + delta)

    slabs = (4, 3, 5, 2, 6, 1, 7, 0)
    gy_at = links.slot(8 * 6)

    def slab_start(s, dy):
        zz = (z + slabs[s]) % 8
        return pl.multiple_of(((y + dy + 4) % 4) * 1024 + (zz % 2) * 512 + (zz // 2) * 128, 128)

    def slab_half(s, dy, h):
        return pl.ds(pl.multiple_of(slab_start(s, dy) + h * 64, 64), 64)

    def weight_slab(s):
        order = (2, 1, -1, 0)
        lhs = jnp.concatenate([cotb[:, :, pl.ds(slab_start(s, dy), 128)] for dy in order], axis=2)
        out = lax.dot_general(lhs.reshape(8 * TOK, 512), gat[...].reshape(8 * TOK, COLS),
                              (((0,), (0,)), ((), ())), preferred_element_type=F32)
        for i, dy in enumerate(order[:3]):
            gwp[pl.ds(slab_start(s, dy), 128), :] = out[i * 128:(i + 1) * 128].astype(BF16)
        vsum[s] = out[384:512]
        base = gy_at + s * 6
        links.send(gwp.at[slab_half(s, 2, 0), :], ra.at[s], base, along_y(1))
        links.send(gwp.at[slab_half(s, 2, 1), :], rb.at[s], base + 1, along_y(-1))
        links.send(gwp.at[slab_half(s, 1, 1), :], half_of(from_lo, s, 1), base + 2, along_y(1))
        links.send(gwp.at[slab_half(s, -1, 0), :], half_of(from_hi, s, 0), base + 3, along_y(-1))

    def half_of(ref, s, h):
        return ref.at[s, pl.ds(h * 64, 64), :]

    def add_slab(s):
        base = gy_at + s * 6
        for dy, h, term, dst, at in ((1, 0, ra, from_lo, 0), (-1, 1, rb, from_hi, 1)):
            links.wait(term.at[s], base + at)
            rows = slab_half(s, dy, h)
            gwp[rows, :] = (gwp[rows, :].astype(F32) + term[s].astype(F32)).astype(BF16)
            links.send(gwp.at[rows, :], half_of(dst, s, h), base + 4 + at, along_y(dy))

    gz_at = links.slot(7)

    def send_slab(s):
        base = gy_at + s * 6
        links.wait(half_of(from_lo, s, 1), base + 2)
        links.wait(half_of(from_hi, s, 0), base + 3)
        links.wait(half_of(from_lo, s, 0), base + 4)
        links.wait(half_of(from_hi, s, 1), base + 5)
        delta = slabs[s]
        total = vsum[s] + from_lo[s].astype(F32) + from_hi[s].astype(F32)
        if delta:
            zsend[delta - 1] = total.astype(BF16)
            links.send(zsend.at[delta - 1], zrecv.at[delta - 1], gz_at + delta - 1, along_z(delta))
        else:
            fin[...] = total

    for s in range(4):
        weight_slab(s)

    def grad_gate(t0, tile, k, rows, lanes):
        grad = grecv[tile // 4, rows, pl.ds((k % 4) * 128, 128)].astype(F32)
        gq[rows, lanes] = (grad * get(cs, t0, tile)).astype(BF16)
        put(gs, t0, tile, (grad * qb[rows, lanes].astype(F32)).astype(BF16).astype(F32))

    blocks = [(x + dx) % 4 for dx in (0, 1, 3, 2)]
    t_at = links.slot(12)
    for turn, block in enumerate(blocks):
        for c in range(2):
            links.wait(grecv.at[block * 2 + c], g_at + block * 2 + c)
        each_tile(grad_gate, block)
        run_states(gs, True, es2, block)
        send_states(-1, es2, er2, t_at, block, turn)
        add_slab(turn)
        weight_slab(4 + turn)
    out_at = links.slot(3)
    links.local(gq, gq_hbm, out_at)

    send_slab(0)
    send_slab(1)
    part = 4

    def adjoint(block):
        for m in range(0, MODES, part):
            rate = par[block, m:m + part]
            decay, growth = jnp.exp(-rate), jnp.exp(rate)
            weight = par[block, MODES + m:MODES + m + part]

            def step(i, carried):
                p, s, da, db = carried
                for r in range(8):
                    rows = row_at(TOK - 1 - (i * 8 + r), block)
                    xt = xs[rows, :][None]
                    p = p * decay + gs[rows, :][None]
                    da = da + p * xt
                    s = (s - xt) * growth
                    db = db + p * s
                    out = tree(p * weight)
                    if m:
                        out = out + cs[rows, :]
                    cs[rows, :] = out
                return p, s, da, db

            zero = jnp.zeros((part, 8, 128), F32)
            start = (carry[block, m:m + part], yend[block, m:m + part], zero, zero)
            _, _, da, db = lax.fori_loop(0, TOK // 8, step, start)
            ab[block, m:m + part] = da
            ab[block, MODES + m:MODES + m + part] = db * decay

    tp_at = links.slot(28)
    for turn, block in enumerate(blocks):
        gather_states(-1, er2, t_at, block, turn)
        adjoint(block)
        for delta in range(1, 8):
            to = pl.ds(((b + delta) % 8) * 4, 4)
            links.send(ab.at[block, to], tp_recv.at[delta - 1, block], tp_at + (delta - 1) * 4 + block,
                       group(delta))
        add_slab(4 + turn)
        send_slab(2 + turn)

    def grads(t0, tile, k, rows, lanes):
        grad = get(cs, t0, tile).astype(BF16).astype(F32)
        gk[rows, lanes] = (grad * vb[rows, lanes].astype(F32)).astype(BF16)
        gv[rows, lanes] = (grad * kb[rows, lanes].astype(F32)).astype(BF16)

    each_block(lambda block: each_tile(grads, block))
    links.local(gk, gk_hbm, out_at + 1)
    links.local(gv, gv_hbm, out_at + 2)

    r1[...] = ab[:, pl.ds(b * 4, 4)]
    for delta in range(1, 8):
        for block in range(4):
            links.wait(tp_recv.at[delta - 1, block], tp_at + (delta - 1) * 4 + block)
        r1[...] += tp_recv[delta - 1]
    c_at = links.slot(3)
    for delta in range(1, 4):
        links.send(r1.at[(zh + delta) % 4], ctx_recv.at[delta - 1], c_at + delta - 1, (f, (zh + delta) % 4))

    send_slab(6)
    send_slab(7)

    for delta in range(1, 8):
        links.wait(zrecv.at[delta - 1], gz_at + delta - 1)
        fin[...] += zrecv[delta - 1].astype(F32)
    fin_at = links.slot(2)
    for h in range(2):
        here = jnp.logical_and(x == zh, core == h)
        src = fin.at[pl.ds(h * 64, 64), :]
        links.send(src, gwo.at[core], fin_at + core, crossed(h), only=jnp.logical_not(here))
        links.local(src, gwo.at[core], fin_at + core, only=here)

    r2[...] = r1[zh]
    for delta in range(1, 4):
        links.wait(ctx_recv.at[delta - 1], c_at + delta - 1)
        r2[...] += ctx_recv[delta - 1]
    o_at = links.slot(7)
    for delta in range(1, 8):
        links.send(r2, g_recv.at[delta - 1], o_at + delta - 1, outer(delta))

    for delta in range(1, 8):
        links.wait(g_recv.at[delta - 1], o_at + delta - 1)
    total = jnp.zeros((4, 8, 128), F32)
    for source in range(8):
        delta = (g + 8 - source) % 8
        theirs = g_recv[jnp.maximum(delta - 1, 0)]
        total = total + jnp.where(delta == 0, r2[...], theirs)
    r3[...] = total
    e_at = links.slot(8)
    for delta in range(1, 8):
        links.send(r3, tot.at[pl.ds(b * 4, 4)], e_at + delta, group(delta))
    links.local(r3, tot.at[pl.ds(b * 4, 4)], e_at)

    gwo_at = links.slot(2)
    for h in range(2):
        links.wait(gwo.at[h], fin_at + h)
        links.local(gwo.at[h], gw_hbm.at[:, pl.ds(h * COLS, COLS)], gwo_at + h)
    for delta in range(8):
        links.wait(tot.at[pl.ds(((b + 8 - delta) % 8) * 4, 4)], e_at + delta)
    ab_at = links.slot(1)
    links.local(tot, ab_hbm, ab_at)

    links.wait(gq, out_at)
    links.wait(gk, out_at + 1)
    links.wait(gv, out_at + 2)
    for h in range(2):
        links.wait(gwo.at[h], gwo_at + h)
    links.wait(tot, ab_at)
    links.finish()


def shards(q_feat, k_feat, v_feat, residue, rate, w_out, cotangent):
    params = jnp.concatenate([rate.T, residue.T], axis=0).reshape(2 * MODES, 8, 128)
    anyspace = pl.BlockSpec(memory_space=pl.ANY)
    flat = (TOK, WIDTH)
    act = jax.ShapeDtypeStruct(flat, BF16)
    v = pltpu.VMEM
    grad_q, grad_k, grad_v, grad_weight, sums = pl.pallas_call(
        kernel,
        out_shape=(act, act, act, jax.ShapeDtypeStruct((64, 1024), F32),
                   jax.ShapeDtypeStruct((2 * MODES, 8, 128), F32)),
        in_specs=[anyspace] * 6,
        out_specs=[anyspace] * 5,
        scratch_shapes=[
            v(flat, BF16), v(flat, BF16), v(flat, BF16),
            v((4, 2 * MODES, 8, 128), F32),
            v((8, TOK, WIDTH), BF16), v((WIDTH, COLS), BF16),
            v((WIDTH, 128), F32), v((WIDTH, 128), F32), v((WIDTH, 128), F32),
            v((512, 128), BF16), v((3, 512, 128), BF16),
            v((512, 128), BF16), v((3, 512, 128), BF16),
            v((4, MODES, 8, 128), F32), v((4, MODES, 8, 128), F32),
            v((8, TOK, COLS), BF16), v((8, TOK, COLS), BF16),
            v((8, TOK, COLS), BF16), v((8, TOK, COLS), BF16),
            v((WIDTH, COLS), BF16),
            v((8, 64, COLS), BF16), v((8, 64, COLS), BF16),
            v((8, 128, COLS), BF16), v((8, 128, COLS), BF16),
            v((8, 128, COLS), F32),
            v((7, 128, COLS), BF16), v((7, 128, COLS), BF16),
            v((128, COLS), F32), v((2, 64, COLS), F32),
            v((4, 2 * MODES, 8, 128), F32),
            v((7, 4, 4, 8, 128), F32), v((4, 4, 8, 128), F32),
            v((3, 4, 8, 128), F32), v((4, 8, 128), F32),
            v((7, 4, 8, 128), F32), v((4, 8, 128), F32),
            v((2 * MODES, 8, 128), F32),
            v(flat, BF16), v(flat, BF16), v(flat, BF16),
            pltpu.SemaphoreType.DMA((N_SEND,)),
            pltpu.SemaphoreType.DMA((N_RECV,)),
        ],
        compiler_params=pltpu.CompilerParams(
            collective_id=0, has_side_effects=True, vmem_limit_bytes=60 * 1024 * 1024),
    )(q_feat[0], k_feat[0], v_feat[0], params, w_out, cotangent[0])
    sums = sums.reshape(2, MODES, 1024)
    grad_residue = sums[0].T
    grad_rate = -residue * sums[1].T
    return grad_q[None], grad_k[None], grad_v[None], grad_weight, grad_residue, grad_rate


def solution(mesh):
    act, modes, proj = P("fsdp", "ctx", None), P("ctx", None), P("fsdp", "ctx")
    return jax.shard_map(
        shards,
        mesh=mesh,
        in_specs=(act, act, act, modes, modes, proj, act),
        out_specs=(act, act, act, proj, modes, modes),
        check_vma=False,
    )
```

time: 195 us -> 158 us (0.81); the launches traced: 191 us -> 157 us
  Pallas kernels: 181 us -> 146 us
    pallas_call x1, Pallas kernels: 181 us -> 146 us  [shards(): pl.pallas_call(kernel, out_shape=(act, act, act, jax.ShapeDtypeStruct((64...]
where the time goes in v2:
time: 158 us; the launch traced here: 157 us
  Pallas kernels  146 us (92%)
  local copies, waits for them, and re-layouts  8.02 us (5%)
    pallas_call x1, Pallas kernels, shards(): pl.pallas_call(kernel, out_shape=(act, act, act, jax.ShapeDtypeStruct((64...  146 us
    unnamed x14, local copies, waits for them, and re-layouts  7.1 us

profile of v2, /device:TPU:3, one launch (start us, length us, event | category | flops | bytes accessed | tf_op | source)
XLA Modules:
  0.0 156.5 jit_solution(1296622714654139427)
XLA Ops:
  0.6 0.9 maximum_bitcast_fusion
  1.5 0.7 copy.13
  2.2 146.3 %shard_map.118 = (bf16[128,4096]{1,0:T(8,128)(2,1)}, bf16[128,4096]{1,0:T(8,128)(2,1)}, bf16[128,4096]{1,0:T(8,128)(2,1)}, f32[64,1024]{1,0:T(8,128)}, f32[32,8,128]{2,1,0:T(8,128)}) custom-call(bf16[128,4096]{1,0:T(8,128)(2,1)} %bitcast.28, bf16[128,4096]{1,0:T(8,128)(2,1)} %bitcast.29, bf16[128,4096]{1,0:T(8,128)(2,1)} %bitcast.30, ...), custom_call_target="tpu_custom_call" | custom-call | tf_op jit(solution)/shard_map/pallas_call | solution.py:598
  148.5 0.0 copy-start.3
  148.5 0.9 fusion.1
  149.4 0.0 copy-done.3
  149.4 0.6 fusion
  150.1 0.6 copy.18
  150.7 0.0 copy-start.1
  150.7 2.4 %copy.23 = bf16[1,128,4096]{2,1,0:T(8,128)(2,1)} copy(bf16[1,128,4096]{2,1,0:T(8,128)(2,1)} %bitcast.34) | data formatting | bytes 2097152
  153.1 0.0 copy-done.1
  153.1 0.0 copy-start
  153.1 1.0 copy.24
  154.1 0.6 copy-done
  154.7 0.0 copy-start.2
  154.7 1.0 copy.25
  155.7 0.1 copy-done.2
  155.8 0.7 copy.26
Async XLA Ops:
  148.5 0.9 copy-start.3
  150.7 2.4 %copy-start.1 = (bf16[128,4096]{1,0:T(8,128)(2,1)S(1)}, bf16[128,4096]{1,0:T(8,128)(2,1)}, u32[]{:S(2)}) copy-start(bf16[128,4096]{1,0:T(8,128)(2,1)} %get-tuple-element.12) | copy-start | bytes 3145732
  153.1 1.6 %copy-start = (bf16[128,4096]{1,0:T(8,128)(2,1)S(1)}, bf16[128,4096]{1,0:T(8,128)(2,1)}, u32[]{:S(2)}) copy-start(bf16[128,4096]{1,0:T(8,128)(2,1)} %get-tuple-element.13) | copy-start | bytes 3145732
  154.7 1.1 copy-start.2

commit v3 on v2

--- a/solution.py
+++ b/solution.py
@@ -58,9 +58,9 @@
                 pl.when(only)(copy.wait_send)
 
 
-def kernel(q_hbm, k_hbm, v_hbm, par_hbm, w_hbm, cot_hbm,
-           gq_hbm, gk_hbm, gv_hbm, gw_hbm, ab_hbm,
-           qb, kb, vb, par, cotb, wbuf, xs, cs, gs, es, er, es2, er2, carry, yend,
+def kernel(q_hbm, k_hbm, v_hbm, rate_hbm, res_hbm, w_hbm, cot_hbm,
+           gq_hbm, gk_hbm, gv_hbm, gw_hbm, gres_hbm, grate_hbm,
+           qb, kb, vb, modes, gmodes, par, cotb, wbuf, xs, cs, gs, es, er, es2, er2, carry, yend,
            gat_send, gat, gsend, grecv, gwp, ra, rb, from_lo, from_hi, vsum,
            zsend, zrecv, fin, gwo, ab, tp_recv, r1, ctx_recv, r2, g_recv, r3, tot,
            gq, gk, gv, send_sems, recv_sems):
@@ -110,8 +110,9 @@
     own = cotb.at[b]
     cot_at = links.slot(1)
     links.local(cot_hbm, own, cot_at)
-    own_par_at = links.slot(1)
-    links.local(par_hbm, par.at[zh], own_par_at)
+    own_par_at = links.slot(2)
+    links.local(rate_hbm, modes.at[0], own_par_at)
+    links.local(res_hbm, modes.at[1], own_par_at + 1)
 
     links.wait(kb, load_at)
     links.wait(vb, load_at + 1)
@@ -146,6 +147,11 @@
 
     each_block(lambda block: each_tile(mix, block))
 
+    for i in range(2):
+        links.wait(modes.at[i], own_par_at + i)
+        for s in range(8):
+            par[zh, i * MODES:(i + 1) * MODES, s, :] = modes[i, :, s * 128:(s + 1) * 128]
+
     @pl.when(x != zh)
     def _():
         pl.semaphore_wait(barrier, len(peers) + 2)
@@ -168,7 +174,7 @@
         links.send(src, wbuf.at[w_rows, :], w_at + core, crossed(h), only=jnp.logical_not(here))
         links.local(src, wbuf.at[w_rows, :], w_at + core, only=here)
     for delta in range(1, 4):
-        links.send(par_hbm.at[pl.ds(core * MODES, MODES)], par_half(zh, core), par_at + delta - 1,
+        links.send(par_half(zh, core), par_half(zh, core), par_at + delta - 1,
                    (f, (zh + delta) % 4))
 
     half = TOK // 2
@@ -238,7 +244,6 @@
         links.send(par_half(source, core), par_half(source, core), sib_par_at + delta - 1, sibling)
     for delta in range(1, 4):
         links.wait(par_half((zh + 4 - delta) % 4, 1 - core), sib_par_at + delta - 1)
-    links.wait(par.at[zh], own_par_at)
 
     def row_at(t, block):
         return pl.ds(pl.multiple_of(t * TILES + block * 8, 8), 8)
@@ -347,6 +352,10 @@
     pass_y(-2)
     pass_y(2)
 
+    gat_at = links.slot(8)
+    links.local(gat_send.at[b], gat.at[b], gat_at)
+    for delta in range(1, 8):
+        links.send(gat_send.at[(b + delta) % 8], gat.at[b], gat_at + delta, group(delta))
     wait_z(4)
     send_y(4)
     pass_y(-3)
@@ -359,10 +368,6 @@
     for h in range(2):
         links.wait(rows_of(cotb.at[far], h), far_at + h)
         share(far, h, 5 + h)
-    gat_at = links.slot(8)
-    links.local(gat_send.at[b], gat.at[b], gat_at)
-    for delta in range(1, 8):
-        links.send(gat_send.at[(b + delta) % 8], gat.at[b], gat_at + delta, group(delta))
     for dz in range(8):
         wait_y(dz)
 
@@ -577,32 +582,38 @@
         links.local(gwo.at[h], gw_hbm.at[:, pl.ds(h * COLS, COLS)], gwo_at + h)
     for delta in range(8):
         links.wait(tot.at[pl.ds(((b + 8 - delta) % 8) * 4, 4)], e_at + delta)
-    ab_at = links.slot(1)
-    links.local(tot, ab_hbm, ab_at)
+    for s in range(8):
+        lanes = slice(s * 128, (s + 1) * 128)
+        gmodes[0, :, lanes] = tot[0:MODES, s, :]
+        gmodes[1, :, lanes] = -modes[1, :, lanes] * tot[MODES:2 * MODES, s, :]
+    ab_at = links.slot(2)
+    links.local(gmodes.at[0], gres_hbm, ab_at)
+    links.local(gmodes.at[1], grate_hbm, ab_at + 1)
 
     links.wait(gq, out_at)
     links.wait(gk, out_at + 1)
     links.wait(gv, out_at + 2)
     for h in range(2):
         links.wait(gwo.at[h], gwo_at + h)
-    links.wait(tot, ab_at)
+    for i in range(2):
+        links.wait(gmodes.at[i], ab_at + i)
     links.finish()
 
 
 def shards(q_feat, k_feat, v_feat, residue, rate, w_out, cotangent):
-    params = jnp.concatenate([rate.T, residue.T], axis=0).reshape(2 * MODES, 8, 128)
     anyspace = pl.BlockSpec(memory_space=pl.ANY)
     flat = (TOK, WIDTH)
     act = jax.ShapeDtypeStruct(flat, BF16)
     v = pltpu.VMEM
-    grad_q, grad_k, grad_v, grad_weight, sums = pl.pallas_call(
+    modes = jax.ShapeDtypeStruct((MODES, 1024), F32)
+    grad_q, grad_k, grad_v, grad_weight, grad_residue, grad_rate = pl.pallas_call(
         kernel,
-        out_shape=(act, act, act, jax.ShapeDtypeStruct((64, 1024), F32),
-                   jax.ShapeDtypeStruct((2 * MODES, 8, 128), F32)),
-        in_specs=[anyspace] * 6,
-        out_specs=[anyspace] * 5,
+        out_shape=(act, act, act, jax.ShapeDtypeStruct((64, 1024), F32), modes, modes),
+        in_specs=[anyspace] * 7,
+        out_specs=[anyspace] * 6,
         scratch_shapes=[
             v(flat, BF16), v(flat, BF16), v(flat, BF16),
+            v((2, MODES, 1024), F32), v((2, MODES, 1024), F32),
             v((4, 2 * MODES, 8, 128), F32),
             v((8, TOK, WIDTH), BF16), v((WIDTH, COLS), BF16),
             v((WIDTH, 128), F32), v((WIDTH, 128), F32), v((WIDTH, 128), F32),
@@ -628,11 +639,8 @@
         ],
         compiler_params=pltpu.CompilerParams(
             collective_id=0, has_side_effects=True, vmem_limit_bytes=60 * 1024 * 1024),
-    )(q_feat[0], k_feat[0], v_feat[0], params, w_out, cotangent[0])
-    sums = sums.reshape(2, MODES, 1024)
-    grad_residue = sums[0].T
-    grad_rate = -residue * sums[1].T
-    return grad_q[None], grad_k[None], grad_v[None], grad_weight, grad_residue, grad_rate
+    )(q_feat[0], k_feat[0], v_feat[0], rate.T, residue.T, w_out, cotangent[0])
+    return grad_q[None], grad_k[None], grad_v[None], grad_weight, grad_residue.T, grad_rate.T
 
 
 def solution(mesh):

time: 158 us -> 154 us (0.975)
    unnamed x14 -> x16, local copies, waits for them, and re-layouts: 7.1 us -> 7.43 us
where the time goes in v3:
time: 154 us
  Pallas kernels  146 us (95%)
  local copies, waits for them, and re-layouts  7.43 us (5%)
    pallas_call x1, Pallas kernels, shards(): pl.pallas_call(kernel, out_shape=(act, act, act, jax.ShapeDtypeStruct((64...  146 us
    unnamed x16, local copies, waits for them, and re-layouts  7.43 us

profile of v3, /device:TPU:3, one launch (start us, length us, event | category | flops | bytes accessed | tf_op | source)
XLA Modules:
  0.0 153.8 jit_solution(3448188308577245275)
XLA Ops:
  0.6 145.8 %shard_map.118 = (bf16[128,4096]{1,0:T(8,128)(2,1)}, bf16[128,4096]{1,0:T(8,128)(2,1)}, bf16[128,4096]{1,0:T(8,128)(2,1)}, f32[64,1024]{1,0:T(8,128)}, f32[16,1024]{1,0:T(8,128)}, /*index=5*/f32[16,1024]{1,0:T(8,128)}) custom-call(bf16[128,4096]{1,0:T(8,128)(2,1)} %bitcast.11, bf16[128,4096]{1,0:T(8,128)(2,1)} %bitcast.12, bf16[128,4096]{1,0:T(8,128)(2,1)} %bitcast.13, ...), custom_call_target="tpu_custom_call" | custom-call | tf_op jit(solution)/shard_map/pallas_call | solution.py:609
  146.4 0.0 copy-start.1
  146.4 2.4 %copy.19 = bf16[1,128,4096]{2,1,0:T(8,128)(2,1)} copy(bf16[1,128,4096]{2,1,0:T(8,128)(2,1)} %bitcast.17) | data formatting | bytes 2097152
  148.8 0.0 copy-done.1
  148.8 0.0 copy-start
  148.8 1.0 copy.20
  149.8 0.6 copy-done
  150.4 0.0 copy-start.2
  150.4 1.0 copy.21
  151.4 0.1 copy-done.2
  151.5 0.0 copy-start.4
  151.5 0.7 copy.22
  152.2 0.2 copy-done.4
  152.3 0.0 copy-start.3
  152.4 0.6 copy.23
  153.0 0.2 copy-done.3
  153.2 0.6 copy.24
Async XLA Ops:
  146.4 2.4 %copy-start.1 = (bf16[128,4096]{1,0:T(8,128)(2,1)S(1)}, bf16[128,4096]{1,0:T(8,128)(2,1)}, u32[]{:S(2)}) copy-start(bf16[128,4096]{1,0:T(8,128)(2,1)} %get-tuple-element.13) | copy-start | bytes 3145732
  148.8 1.6 %copy-start = (bf16[128,4096]{1,0:T(8,128)(2,1)S(1)}, bf16[128,4096]{1,0:T(8,128)(2,1)}, u32[]{:S(2)}) copy-start(bf16[128,4096]{1,0:T(8,128)(2,1)} %get-tuple-element.14) | copy-start | bytes 3145732
  150.4 1.1 copy-start.2
  151.5 0.9 copy-start.4
  152.3 0.9 copy-start.3

commit v4 on v3

--- a/solution.py
+++ b/solution.py
@@ -392,20 +392,15 @@
 
     links.wait(own, cot_at)
     links.wait(cotb.at[b + other], sib_at)
-    project(x)
-    return_chip(0)
     links.wait(rows_of(cotb.at[left + other], 0), sib_at + 1)
     links.wait(rows_of(cotb.at[left + other], 1), sib_at + 3)
-    project((x + 3) % 4)
-    return_chip(3)
     links.wait(rows_of(cotb.at[right + other], 1), sib_at + 2)
     links.wait(rows_of(cotb.at[right + other], 0), sib_at + 4)
-    project((x + 1) % 4)
-    return_chip(1)
     for h in range(2):
         links.wait(rows_of(cotb.at[far + other], h), sib_at + 5 + h)
-    project((x + 2) % 4)
-    return_chip(2)
+    for dx in (2, 3, 1, 0):
+        project((x + dx) % 4)
+        return_chip(dx)
 
     for delta in range(8):
         links.wait(gat.at[(b + 8 - delta) % 8], gat_at + delta)
@@ -469,7 +464,7 @@
         gq[rows, lanes] = (grad * get(cs, t0, tile)).astype(BF16)
         put(gs, t0, tile, (grad * qb[rows, lanes].astype(F32)).astype(BF16).astype(F32))
 
-    blocks = [(x + dx) % 4 for dx in (0, 1, 3, 2)]
+    blocks = [(x + dx) % 4 for dx in (2, 1, 3, 0)]
     t_at = links.slot(12)
     for turn, block in enumerate(blocks):
         for c in range(2):

time: 154 us -> 155 us (level)
  no operation moved by 1% of the time
where the time goes in v4:
time: 155 us; the launch traced here: 154 us
  Pallas kernels  146 us (94%)
  local copies, waits for them, and re-layouts  7.43 us (5%)
    pallas_call x1, Pallas kernels, shards(): pl.pallas_call(kernel, out_shape=(act, act, act, jax.ShapeDtypeStruct((64...  146 us
    unnamed x16, local copies, waits for them, and re-layouts  7.43 us

profile of v4, /device:TPU:3, one launch (start us, length us, event | category | flops | bytes accessed | tf_op | source)
XLA Modules:
  0.0 154.0 jit_solution(13167720672205468270)
XLA Ops:
  0.6 146.0 %shard_map.118 = (bf16[128,4096]{1,0:T(8,128)(2,1)}, bf16[128,4096]{1,0:T(8,128)(2,1)}, bf16[128,4096]{1,0:T(8,128)(2,1)}, f32[64,1024]{1,0:T(8,128)}, f32[16,1024]{1,0:T(8,128)}, /*index=5*/f32[16,1024]{1,0:T(8,128)}) custom-call(bf16[128,4096]{1,0:T(8,128)(2,1)} %bitcast.11, bf16[128,4096]{1,0:T(8,128)(2,1)} %bitcast.12, bf16[128,4096]{1,0:T(8,128)(2,1)} %bitcast.13, ...), custom_call_target="tpu_custom_call" | custom-call | tf_op jit(solution)/shard_map/pallas_call | solution.py:604
  146.6 0.0 copy-start.1
  146.6 2.4 %copy.19 = bf16[1,128,4096]{2,1,0:T(8,128)(2,1)} copy(bf16[1,128,4096]{2,1,0:T(8,128)(2,1)} %bitcast.17) | data formatting | bytes 2097152
  149.0 0.0 copy-done.1
  149.0 0.0 copy-start
  149.0 1.0 copy.20
  150.0 0.6 copy-done
  150.6 0.0 copy-start.2
  150.6 1.0 copy.21
  151.6 0.1 copy-done.2
  151.7 0.0 copy-start.4
  151.7 0.7 copy.22
  152.4 0.2 copy-done.4
  152.5 0.0 copy-start.3
  152.5 0.6 copy.23
  153.2 0.2 copy-done.3
  153.4 0.6 copy.24
Async XLA Ops:
  146.6 2.4 %copy-start.1 = (bf16[128,4096]{1,0:T(8,128)(2,1)S(1)}, bf16[128,4096]{1,0:T(8,128)(2,1)}, u32[]{:S(2)}) copy-start(bf16[128,4096]{1,0:T(8,128)(2,1)} %get-tuple-element.13) | copy-start | bytes 3145732
  149.0 1.6 %copy-start = (bf16[128,4096]{1,0:T(8,128)(2,1)S(1)}, bf16[128,4096]{1,0:T(8,128)(2,1)}, u32[]{:S(2)}) copy-start(bf16[128,4096]{1,0:T(8,128)(2,1)} %get-tuple-element.14) | copy-start | bytes 3145732
  150.6 1.1 copy-start.2
  151.7 0.9 copy-start.4
  152.5 0.9 copy-start.3
